TPU v7x, 512 devices: a whole 4x4x16 slice. The times are simulated.
512 devices in a mesh: row: 32 (over z, core), col: 16 (over x, y).
Axes of the slice: x: 4, y: 4, z: 16, core: 2. Of those that a mesh axis runs over, the one named last changes fastest.
Arguments:
- inputs: bfloat16 [256, 12288], P('col', 'row'), may hold values from -6 to 6
- w_in: bfloat16 [12288, 24576], P('row', 'col'), may hold values from -0.0546875 to 0.0546875
- w_out: bfloat16 [24576, 12288], P('col', 'row'), may hold values from -0.0390625 to 0.0390625
- cotangent: bfloat16 [256, 12288], P('col', 'row'), may hold values from -1.5 to 1.5
Outputs:
- output: bfloat16 [256, 12288], P('col', 'row')
- input_grad: bfloat16 [256, 12288], P('col', 'row')
- w_in_grad: bfloat16 [12288, 24576], P('row', 'col')
- w_out_grad: bfloat16 [24576, 12288], P('col', 'row')
All inputs are finite; a program needn't handle non-finite values.
Results may differ from a plain program's by a relative error of at most 0.005.
Values may be sent and summed in bfloat16 or wider, within the bound.
A program may use at most 64 MiB of HBM per device.

v0:
```python
import jax
import jax.numpy as jnp
from jax import lax
from jax.sharding import PartitionSpec as P

gelu_coef = 0.7978845608
cubic_coef = 0.044715


def gelu_tanh(value):
    return 0.5 * value * (1.0 + jnp.tanh(gelu_coef * (value + cubic_coef * value * value * value)))


def gelu_slope(value):
    inner = jnp.tanh(gelu_coef * (value + cubic_coef * value * value * value))
    return 0.5 * (1.0 + inner) + 0.5 * value * (1.0 - inner * inner) * gelu_coef * (
        1.0 + 3.0 * cubic_coef * value * value
    )


def contract_last(left, right):
    return lax.dot_general(
        left, right, (((1,), (1,)), ((), ())), preferred_element_type=jnp.float32
    )


def contract_first(left, right):
    return lax.dot_general(
        left, right, (((0,), (0,)), ((), ())), preferred_element_type=jnp.float32
    )


def local(inputs, w_in, w_out, cotangent):
    tokens_all = lax.all_gather(inputs, "col", axis=0, tiled=True)
    piece = tokens_all
    pre_share = lax.psum_scatter(
        jnp.dot(piece, w_in, preferred_element_type=jnp.float32),
        "row",
        scatter_dimension=0,
        tiled=True,
    )
    hidden_share = gelu_tanh(pre_share).astype(jnp.bfloat16)
    hidden_all = lax.all_gather(hidden_share, "row", axis=0, tiled=True)
    piece = hidden_all
    output = lax.psum_scatter(
        jnp.dot(piece, w_out, preferred_element_type=jnp.float32),
        "col",
        scatter_dimension=0,
        tiled=True,
    ).astype(jnp.bfloat16)
    grad_all = lax.all_gather(cotangent, "col", axis=0, tiled=True)
    w_out_grad = contract_first(hidden_all, grad_all).astype(jnp.bfloat16)
    piece = grad_all
    grad_share = lax.psum_scatter(
        contract_last(piece, w_out), "row", scatter_dimension=0, tiled=True
    )
    pre_grad_share = (grad_share * gelu_slope(pre_share)).astype(jnp.bfloat16)
    pre_grad = lax.all_gather(pre_grad_share, "row", axis=0, tiled=True)
    w_in_grad = contract_first(tokens_all, pre_grad).astype(jnp.bfloat16)
    piece = pre_grad
    input_grad = lax.psum_scatter(
        contract_last(piece, w_in), "col", scatter_dimension=0, tiled=True
    ).astype(jnp.bfloat16)
    return (output, input_grad, w_in_grad, w_out_grad)


def solution(mesh):
    placed = (P("col", "row"), P("row", "col"), P("col", "row"), P("col", "row"))
    return jax.shard_map(
        local,
        mesh=mesh,
        in_specs=placed,
        out_specs=(P("col", "row"), P("col", "row"), P("row", "col"), P("col", "row")),
        check_vma=False,
    )
```

profile of v0, /device:TPU:32, one launch (start us, length us, event | category | flops | bytes accessed | tf_op | source)
XLA Modules:
  0.0 411.8 jit_solution(13061587322046206071)
XLA Ops:
  7.2 0.0 copy-start
  7.2 0.0 reduce-scatter.3.cloned.1.call-start
  7.2 24.2 %all_gather.12 = bf16[256,384]{1,0:T(8,128)(2,1)S(1)} all-gather(bf16[16,384]{1,0:T(8,128)(2,1)} %param.4), channel_id=1, replica_groups=mesh['row'=32,'col'=16] {'col'}, dimensions={0}, use_global_device_ids=true | all-gather | bytes 208896 | tf_op jit(solution)/shard_map/all_gather | solution.py:34
  31.4 0.0 copy-start.2
  31.4 0.7 copy-done.2
  32.1 0.0 copy-done
  32.1 1.7 fusion.8
  33.8 0.0 copy-start.8
  33.8 0.0 copy-start.1
  33.8 0.0 reduce-scatter.3.cloned.1.call-update
  33.9 0.0 reduce-scatter.5.cloned.1.call-start
  33.9 0.6 copy-done.8
  34.5 23.1 %all_gather.14 = bf16[256,384]{1,0:T(8,128)(2,1)S(1)} all-gather(bf16[16,384]{1,0:T(8,128)(2,1)S(1)} %copy-done.8), channel_id=1, replica_groups=mesh['row'=32,'col'=16] {'col'}, dimensions={0}, use_global_device_ids=true | all-gather | bytes 208896 | tf_op jit(solution)/shard_map/all_gather | solution.py:51
  57.6 0.0 copy-done.1
  57.6 0.0 copy-start.4
  57.7 1.8 fusion.10
  59.4 0.0 copy-done.4
  59.4 0.0 reduce-scatter.5.cloned.1.call-update
  59.4 1.3 dynamic-slice
  61.4 80.3 %reduce-scatter.3.cloned.1.call-done = f32[8,1536]{1,0:T(8,128)} async-done(((f32[256,1536]{1,0:T(8,128)}), f32[8,1536]{1,0:T(8,128)}) %reduce-scatter.3.cloned.1.call-update) | async-done | bytes 49168 | tf_op jit(solution)/shard_map/reduce_scatter | solution.py:36
  141.6 110.0 %reduce-scatter.5.cloned.1.call-done = f32[8,1536]{1,0:T(8,128)} async-done(((f32[256,1536]{1,0:T(8,128)}), f32[8,1536]{1,0:T(8,128)}) %reduce-scatter.5.cloned.1.call-update) | async-done | bytes 49168 | tf_op jit(solution)/shard_map/reduce_scatter | solution.py:54
  251.6 0.9 fusion.7
  252.5 32.6 %all_gather.15 = bf16[256,1536]{1,0:T(8,128)(2,1)S(1)} all-gather(bf16[8,1536]{1,0:T(8,128)(2,1)S(1)} %get-tuple-element.14), channel_id=1, replica_groups=mesh['row'=32,'col'=16] {'row'}, dimensions={0}, use_global_device_ids=true | all-gather | bytes 811008 | tf_op jit(solution)/shard_map/all_gather | solution.py:58
  285.2 0.0 copy-start.3
  285.2 1.3 fusion.11
  286.5 0.0 copy-done.3
  286.5 0.6 fusion
  287.1 29.2 %all_gather.13 = bf16[256,1536]{1,0:T(8,128)(2,1)S(1)} all-gather(bf16[8,1536]{1,0:T(8,128)(2,1)S(1)} %get-tuple-element.15), channel_id=1, replica_groups=mesh['row'=32,'col'=16] {'row'}, dimensions={0}, use_global_device_ids=true | all-gather | bytes 811008 | tf_op jit(solution)/shard_map/all_gather | solution.py:43
  316.3 0.0 copy-start.5
  316.3 1.3 fusion.9
  317.6 0.0 copy-done.5
  317.6 1.6 convolution_convert_fusion
  319.3 0.0 copy-start.6
  319.3 0.0 copy-start.7
  319.3 1.4 copy.9
  320.7 0.0 copy-done.6
  320.7 0.0 copy-done.7
  320.7 83.6 %all-reduce.4 = (bf16[256,384]{1,0:T(8,128)(2,1)S(1)}, bf16[256,384]{1,0:T(8,128)(2,1)S(1)}) all-reduce(f32[256,384]{1,0:T(8,128)S(1)} %copy-done.7, f32[256,384]{1,0:T(8,128)S(1)} %copy-done.6), channel_id=3, replica_groups=mesh['row'=32,'col'=16] {'col'}, use_global_device_ids=true, to_apply=%region_1.0.clone | all-reduce | flops 196608 | bytes 1179648
  404.3 0.6 dynamic-slice_convert_fusion
Async XLA Ops:
  7.2 24.9 %copy-start = (bf16[384,1536]{1,0:T(8,128)(2,1)S(1)}, bf16[384,1536]{1,0:T(8,128)(2,1)}, u32[]{:S(2)}) copy-start(bf16[384,1536]{1,0:T(8,128)(2,1)} %param.5) | copy-start | bytes 3538948
  7.2 134.5 %reduce-scatter.3.cloned.1.call-start = ((), (), s32[]{:S(2)}) async-start(), calls=%async_computation.2 | async-start | bytes 1622016 | tf_op jit(solution)/shard_map/reduce_scatter | solution.py:36
  31.4 0.7 copy-start.2
  33.8 0.7 copy-start.8
  33.8 23.8 %copy-start.1 = (bf16[1536,384]{1,0:T(8,128)(2,1)S(1)}, bf16[1536,384]{1,0:T(8,128)(2,1)}, u32[]{:S(2)}) copy-start(bf16[1536,384]{1,0:T(8,128)(2,1)} %param.6) | copy-start | bytes 3538948
  33.9 217.8 %reduce-scatter.5.cloned.1.call-start = ((), (), s32[]{:S(2)}) async-start(), calls=%async_computation.3 | async-start | bytes 1622016 | tf_op jit(solution)/shard_map/reduce_scatter | solution.py:54
  57.6 1.8 copy-start.4
  285.2 1.3 copy-start.3
  316.3 1.3 copy-start.5
  319.3 1.4 copy-start.6
  319.3 1.4 copy-start.7
Sparse Core Ops, SparseCore 0:
  34.0 107.6 reduce-scatter.2
  144.7 106.9 reduce-scatter.4
where the time goes:
time: 412 us
  blocking collectives  193 us (47%)
  waiting for transfers between devices  190 us (46%)
  between operations  14.7 us (4%)
  matrix products  8.32 us (2%)
  local copies, waits for them, and re-layouts  4.67 us (1%)
    reduce_scatter x1, waiting for transfers between devices, local(): lax.psum_scatter(contract_last(piece, w_out), 'row', scatter_dimension=0,...  110 us
    unnamed x1, blocking collectives  83.6 us
    reduce_scatter x1, waiting for transfers between devices, local(): lax.psum_scatter(jnp.dot(piece, w_in, preferred_element_type=jnp.float32)...  80.3 us
    all_gather x1, blocking collectives, local(): pre_grad = lax.all_gather(pre_grad_share, 'row', axis=0, tiled=True)  32.6 us
    all_gather x1, blocking collectives, local(): hidden_all = lax.all_gather(hidden_share, 'row', axis=0, tiled=True)  29.2 us
    all_gather x1, blocking collectives, local(): tokens_all = lax.all_gather(inputs, 'col', axis=0, tiled=True)  24.2 us
    all_gather x1, blocking collectives, local(): grad_all = lax.all_gather(cotangent, 'col', axis=0, tiled=True)  23.1 us
  transfers between devices with their start and end apart: 2, of which 2 were waited for; matrix products, arithmetic and copies ran while one was open for 1% of the time, Pallas kernels for 0%

commit v1 on v0

v1 whole, which is shorter than its diff:
```python
import jax
import jax.numpy as jnp
from jax import lax
from jax.experimental import pallas as pl
from jax.experimental.pallas import tpu as pltpu
from jax.sharding import PartitionSpec as P

MESH = pl.DeviceIdType.MESH
gelu_coef = 0.7978845608
cubic_coef = 0.044715

CHIPS = 16
COLS = 16
BLOCK = 16
TOKENS = 256
DEPTH = 384
UNITS = 1536
HALF = 768

PARENT = {
    3: 0, -3: 0, 1: 0, -1: 0, 6: 3, -6: -3, 4: 3, -4: -3, 2: 1, -2: -1, 8: 6, 7: 6, -7: -6, 5: 4, -5: -4,
}
CHILDREN = {}
for child, parent in PARENT.items():
    CHILDREN.setdefault(parent, []).append(child)
FAR_FIRST = (
    (2, 2), (1, 2), (3, 2), (2, 1), (2, 3), (0, 2), (2, 0), (1, 1), (1, 3), (3, 1), (3, 3), (0, 1), (0, 3), (1, 0), (3, 0),
)
FIRST = (8, 7, -7, 5, -5, 2, -2)
SECOND = (6, -6, 4, -4, 1, -1)
THIRD = (3, -3)
OFFSETS = sorted({PARENT[r] - r for r in PARENT} | {r - PARENT[r] for r in PARENT})
MIDDLE, LOW, HIGH = range(4, 12), range(0, 4), range(12, 16)


def rows(role):
    return pl.ds((role + 7) * BLOCK, BLOCK)


def contract_last(left, right):
    return lax.dot_general(
        left, right, (((1,), (1,)), ((), ())), preferred_element_type=jnp.float32
    )


def contract_first(left, right):
    return lax.dot_general(
        left, right, (((0,), (0,)), ((), ())), preferred_element_type=jnp.float32
    )


def kernel(
    inputs, w_in, w_out, cotangent,
    output, input_grad, w_in_grad, w_out_grad,
    tokens, tokens_twin, w_in_v, w_out_v, w_in_twin, w_out_twin, mine, sums, sums_in, units, send_out, recv_out,
    load_sem, own_sem, gather_send, gather_recv, pair_send, pair_recv, swap_send, swap_recv, sum_send, sum_recv,
    unit_send, unit_recv, twin_send, twin_recv, out_send, out_recv,
):
    row, col = lax.axis_index("row"), lax.axis_index("col")
    z, c = row // 2, lax.rem(row, 2)
    twin = (z * 2 + 1 - c, col)

    def along(offset):
        return (lax.rem(z + offset + CHIPS, CHIPS) * 2 + c, col)

    def across(step):
        return (row, lax.rem(col // 4 + step[0], 4) * 4 + lax.rem(lax.rem(col, 4) + step[1], 4))

    def send(src, dst, send_sem, recv_sem, device):
        pltpu.make_async_remote_copy(
            src_ref=src, dst_ref=dst, send_sem=send_sem, recv_sem=recv_sem,
            device_id=device, device_id_type=MESH,
        ).start()

    def wait(ref, sem):
        pltpu.make_async_copy(ref, ref, sem).wait()

    here = pl.ds(pl.multiple_of(lax.rem(z - col + 7 + CHIPS, CHIPS) * BLOCK, BLOCK), BLOCK)

    own = [
        pltpu.make_async_copy(source, tokens.at[k, here], own_sem.at[k])
        for k, source in enumerate((inputs, cotangent))
    ]
    loads = [
        pltpu.make_async_copy(w_in.at[:, pl.ds(h * HALF, HALF)], w_in_v.at[h], load_sem.at[h])
        for h in range(2)
    ] + [pltpu.make_async_copy(w_out.at[pl.ds(h * HALF, HALF)], w_out_v.at[h], load_sem.at[2 + h]) for h in range(2)]
    for copy in own + loads:
        copy.start()

    barrier = pltpu.get_barrier_semaphore()
    peers = [across(step) for step in FAR_FIRST] + [along(offset) for offset in OFFSETS] + [twin]
    for peer in peers:
        pl.semaphore_signal(barrier, inc=1, device_id=peer, device_id_type=MESH)
    pl.semaphore_wait(barrier, len(peers))

    for k in range(2):
        own[k].wait()
        for step in FAR_FIRST:
            send(tokens.at[k, here], tokens.at[k, here], gather_send.at[k], gather_recv.at[k], across(step))
        if k == 0:
            theirs = w_in.at[:, pl.ds(pl.multiple_of((1 - c) * HALF, HALF), HALF)]
            send(theirs, w_in_twin, swap_send.at[0], swap_recv.at[0], twin)
        else:
            theirs = w_out.at[pl.ds(pl.multiple_of((1 - c) * HALF, HALF), HALF)]
            send(theirs, w_out_twin, swap_send.at[1], swap_recv.at[1], twin)
    for copy in loads:
        copy.wait()

    def first_round(k):
        wait(tokens.at[k, pl.ds(0, (COLS - 1) * BLOCK)], gather_recv.at[k])
        send(tokens.at[k], tokens_twin.at[k], pair_send.at[k], pair_recv.at[k], twin)
        if k == 0:
            mine[0] = jnp.dot(tokens[0], w_in_v[c], preferred_element_type=jnp.float32)
            wait(w_in_twin, swap_recv.at[0])
            wait(tokens_twin.at[0], pair_recv.at[0])
            mine[0] += jnp.dot(tokens_twin[0], w_in_twin[...], preferred_element_type=jnp.float32)
        else:
            mine[1] = contract_last(tokens[1], w_out_v[c])
            wait(w_out_twin, swap_recv.at[1])
            wait(tokens_twin.at[1], pair_recv.at[1])
            mine[1] += contract_last(tokens_twin[1], w_out_twin[...])
        for role in FIRST:
            pass_on(k, role)

    def collected(k, role):
        value = mine[k, rows(role)]
        for child in CHILDREN.get(role, ()):
            wait(sums_in.at[k, rows(child)], sum_recv.at[k, child + 7])
            value = value + sums_in[k, rows(child)].astype(jnp.float32)
        return value

    def pass_on(k, role):
        sums[k, rows(role)] = collected(k, role).astype(jnp.bfloat16)
        send(
            sums.at[k, rows(role)], sums_in.at[k, rows(role)], sum_send.at[k], sum_recv.at[k, role + 7],
            along(PARENT[role] - role),
        )

    def hand_out(k, role):
        for child in CHILDREN.get(role, ()):
            send(
                units.at[k, c, rows(role)], units.at[k, c, rows(child)], unit_send.at[k], unit_recv.at[k, child + 7],
                along(child - role),
            )
        group = 0 if role + 7 in MIDDLE else 1 if role + 7 in LOW else 2
        send(units.at[k, c, rows(role)], units.at[k, c, rows(role)], twin_send.at[k], twin_recv.at[k, group], twin)

    def relay(k, role):
        wait(units.at[k, c, rows(role)], unit_recv.at[k, role + 7])
        hand_out(k, role)

    def unit_terms(k, group, blocks):
        span = pl.ds(blocks[0] * BLOCK, len(blocks) * BLOCK)
        wait(units.at[k, 1 - c, span], twin_recv.at[k, group])
        if k == 0:
            value = jnp.dot(units[0, 0, span], w_out_v[0], preferred_element_type=jnp.float32)
            value = value + jnp.dot(units[0, 1, span], w_out_v[1], preferred_element_type=jnp.float32)
        else:
            value = contract_last(units[1, 0, span], w_in_v[0])
            value = value + contract_last(units[1, 1, span], w_in_v[1])
        send_out[k, span] = value.astype(jnp.bfloat16)
        for p in blocks:
            target = lax.rem(z + 7 - p + CHIPS, CHIPS)
            source = send_out.at[k, pl.ds(p * BLOCK, BLOCK)]

            @pl.when(target != col)
            def _():
                send(source, recv_out.at[k, col], out_send.at[k], out_recv.at[k], (row, target))

            @pl.when(target == col)
            def _():
                recv_out[k, col] = source[...]

    first_round(0)
    first_round(1)
    for k in range(2):
        for role in SECOND:
            pass_on(k, role)
    for k in range(2):
        for role in THIRD:
            pass_on(k, role)

    pre_act = collected(0, 0)
    inner = jnp.tanh(gelu_coef * (pre_act + cubic_coef * pre_act * pre_act * pre_act))
    units[0, c, rows(0)] = (0.5 * pre_act * (1.0 + inner)).astype(jnp.bfloat16)
    hand_out(0, 0)
    slope = 0.5 * (1.0 + inner) + 0.5 * pre_act * (1.0 - inner * inner) * gelu_coef * (
        1.0 + 3.0 * cubic_coef * pre_act * pre_act
    )
    units[1, c, rows(0)] = (collected(1, 0) * slope).astype(jnp.bfloat16)
    hand_out(1, 0)

    for group in (THIRD + (1, -1), (6, -6, 4, -4, 2, -2)):
        for k in range(2):
            for role in group:
                relay(k, role)
    for k in range(2):
        unit_terms(k, 0, MIDDLE)
        for role in (8, 7, -7, 5, -5):
            relay(k, role)
    for k in range(2):
        unit_terms(k, 1, LOW)
        unit_terms(k, 2, HIGH)
    for h in range(2):
        span = pl.ds(h * HALF, HALF)
        w_out_grad[span, :] = contract_first(units[0, h], tokens[1]).astype(jnp.bfloat16)
        w_in_grad[:, span] = contract_first(tokens[0], units[1, h]).astype(jnp.bfloat16)
    for k in range(2):
        wait(recv_out.at[k, pl.ds(0, COLS - 1)], out_recv.at[k])
        value = recv_out[k, 0].astype(jnp.float32)
        for source in range(1, COLS):
            value = value + recv_out[k, source].astype(jnp.float32)
        (output, input_grad)[k][...] = value.astype(jnp.bfloat16)

    for k in range(2):
        span = pl.ds(0, (COLS - 1) * BLOCK)
        wait(tokens.at[k, span], gather_send.at[k])
        wait(tokens_twin.at[k], pair_send.at[k])
        wait(sums.at[k, span], sum_send.at[k])
        wait(units.at[k, 0, span], unit_send.at[k])
        wait(units.at[k, 0], twin_send.at[k])
        wait(send_out.at[k, span], out_send.at[k])
    wait(w_in_twin, swap_send.at[0])
    wait(w_out_twin, swap_send.at[1])


def place(*refs):
    copies = [pltpu.make_async_copy(refs[i], refs[4 + i], refs[8].at[i]) for i in range(4)]
    for copy in copies:
        copy.start()
    for copy in copies:
        copy.wait()


def exchange(inputs, w_in, w_out, cotangent):
    bf16, f32 = jnp.bfloat16, jnp.float32
    dma = pltpu.SemaphoreType.DMA
    hbm, vmem = pl.BlockSpec(memory_space=pltpu.HBM), pl.BlockSpec(memory_space=pltpu.VMEM)
    shape = jax.ShapeDtypeStruct
    return pl.pallas_call(
        kernel,
        out_shape=(
            shape((BLOCK, DEPTH), bf16),
            shape((BLOCK, DEPTH), bf16),
            shape((DEPTH, UNITS), bf16),
            shape((UNITS, DEPTH), bf16),
        ),
        in_specs=[hbm] * 4,
        out_specs=(vmem,) * 4,
        scratch_shapes=[
            pltpu.VMEM((2, TOKENS, DEPTH), bf16),
            pltpu.VMEM((2, TOKENS, DEPTH), bf16),
            pltpu.VMEM((2, DEPTH, HALF), bf16),
            pltpu.VMEM((2, HALF, DEPTH), bf16),
            pltpu.VMEM((DEPTH, HALF), bf16),
            pltpu.VMEM((HALF, DEPTH), bf16),
            pltpu.VMEM((2, TOKENS, HALF), f32),
            pltpu.VMEM((2, TOKENS, HALF), bf16),
            pltpu.VMEM((2, TOKENS, HALF), bf16),
            pltpu.VMEM((2, 2, TOKENS, HALF), bf16),
            pltpu.VMEM((2, TOKENS, DEPTH), bf16),
            pltpu.VMEM((2, COLS, BLOCK, DEPTH), bf16),
            dma((4,)), dma((2,)), dma((2,)), dma((2,)), dma((2,)), dma((2,)), dma((2,)), dma((2,)),
            dma((2,)), dma((2, 16)), dma((2,)), dma((2, 16)), dma((2,)), dma((2, 3)), dma((2,)), dma((2,)),
        ],
        compiler_params=pltpu.CompilerParams(
            collective_id=0, has_side_effects=True, vmem_limit_bytes=40 * 1024 * 1024
        ),
        name="feed_forward",
    )(inputs, w_in, w_out, cotangent)


def local(inputs, w_in, w_out, cotangent):
    results = exchange(inputs, w_in, w_out, cotangent)
    return pl.pallas_call(
        place,
        out_shape=tuple(jax.ShapeDtypeStruct(result.shape, result.dtype) for result in results),
        in_specs=[pl.BlockSpec(memory_space=pltpu.VMEM)] * 4,
        out_specs=(pl.BlockSpec(memory_space=pltpu.HBM),) * 4,
        scratch_shapes=[pltpu.SemaphoreType.DMA((4,))],
        name="place",
    )(*results)


def solution(mesh):
    placed = (P("col", "row"), P("row", "col"), P("col", "row"), P("col", "row"))
    return jax.shard_map(
        local,
        mesh=mesh,
        in_specs=placed,
        out_specs=(P("col", "row"), P("col", "row"), P("row", "col"), P("col", "row")),
        check_vma=False,
    )
```

time: 412 us -> 72.8 us (0.18)
  the two profiles are of different devices: /device:TPU:32 before, /device:TPU:4 now
where the time goes in v1:
time: 72.8 us; the launch traced here: 72.5 us
  Pallas kernels  64.6 us (89%)
  local copies, waits for them, and re-layouts  7.2 us (10%)
    pallas_call x1, Pallas kernels, exchange(): pl.pallas_call(kernel, out_shape=(shape((BLOCK, DEPTH), bf16), shape((BLO...  61.5 us
    unnamed x16, local copies, waits for them, and re-layouts  7.2 us
    pallas_call x1, Pallas kernels, local(): pl.pallas_call(place, out_shape=tuple((jax.ShapeDtypeStruct(result.shape,...  3.1 us

profile of v1, /device:TPU:4, one launch (start us, length us, event | category | flops | bytes accessed | tf_op | source)
XLA Modules:
  0.0 72.5 jit_solution(9629040625035948896)
XLA Ops:
  0.6 0.0 copy-start
  0.6 1.3 %copy-done = bf16[384,1536]{1,0:T(8,128)(2,1)S(1)} copy-done((bf16[384,1536]{1,0:T(8,128)(2,1)S(1)}, bf16[384,1536]{1,0:T(8,128)(2,1)}, u32[]{:S(2)}) %copy-start) | copy-done | bytes 1179672
  1.9 0.0 copy-start.1
  1.9 1.3 %copy-done.1 = bf16[1536,384]{1,0:T(8,128)(2,1)S(1)} copy-done((bf16[1536,384]{1,0:T(8,128)(2,1)S(1)}, bf16[1536,384]{1,0:T(8,128)(2,1)}, u32[]{:S(2)}) %copy-start.1) | copy-done | bytes 1179672
  3.2 0.0 copy-start.4
  3.2 0.7 copy-done.4
  3.9 0.0 copy-start.5
  3.9 0.7 copy-done.5
  4.6 61.5 %feed_forward.1 = (bf16[16,384]{1,0:T(8,128)(2,1)S(1)}, bf16[16,384]{1,0:T(8,128)(2,1)S(1)}, bf16[384,1536]{1,0:T(8,128)(2,1)S(1)}, bf16[1536,384]{1,0:T(8,128)(2,1)S(1)}) custom-call(bf16[16,384]{1,0:T(8,128)(2,1)S(1)} %copy-done.4, bf16[384,1536]{1,0:T(8,128)(2,1)S(1)} %copy-done, bf16[1536,384]{1,0:T(8,128)(2,1)S(1)} %copy-done.1, ...), custom_call_target="tpu_custom_call" | custom-call | tf_op jit(solution)/shard_map/feed_forward/pallas_call | solution.py:241
  66.1 0.0 copy-start.2
  66.1 1.0 %copy-done.2 = bf16[384,1536]{1,0:T(8,128)(2,1)} copy-done((bf16[384,1536]{1,0:T(8,128)(2,1)}, bf16[384,1536]{1,0:T(8,128)(2,1)S(1)}, u32[]{:S(2)}) %copy-start.2) | copy-done | bytes 1179672
  67.2 0.0 copy-start.3
  67.2 1.0 %copy-done.3 = bf16[1536,384]{1,0:T(8,128)(2,1)} copy-done((bf16[1536,384]{1,0:T(8,128)(2,1)}, bf16[1536,384]{1,0:T(8,128)(2,1)S(1)}, u32[]{:S(2)}) %copy-start.3) | copy-done | bytes 1179672
  68.2 0.0 copy-start.6
  68.2 0.6 copy-done.6
  68.8 0.0 copy-start.7
  68.8 0.6 copy-done.7
  69.4 3.1 %place.1 = (bf16[16,384]{1,0:T(8,128)(2,1)}, bf16[16,384]{1,0:T(8,128)(2,1)}, bf16[384,1536]{1,0:T(8,128)(2,1)}, bf16[1536,384]{1,0:T(8,128)(2,1)}) custom-call(bf16[16,384]{1,0:T(8,128)(2,1)} %copy-done.6, bf16[16,384]{1,0:T(8,128)(2,1)} %copy-done.7, bf16[384,1536]{1,0:T(8,128)(2,1)} %copy-done.2, bf16[1536,384]{1,0:T(8,128)(2,1)} %copy-done.3), custom_call_target="tpu_custom_call" | custom-call | tf_op jit(solution)/shard_map/place/pallas_call | solution.py:276
Async XLA Ops:
  0.6 1.3 %copy-start = (bf16[384,1536]{1,0:T(8,128)(2,1)S(1)}, bf16[384,1536]{1,0:T(8,128)(2,1)}, u32[]{:S(2)}) copy-start(bf16[384,1536]{1,0:T(8,128)(2,1)} %w_in.1) | copy-start | bytes 3538948
  1.9 1.3 %copy-start.1 = (bf16[1536,384]{1,0:T(8,128)(2,1)S(1)}, bf16[1536,384]{1,0:T(8,128)(2,1)}, u32[]{:S(2)}) copy-start(bf16[1536,384]{1,0:T(8,128)(2,1)} %w_out.1) | copy-start | bytes 3538948
  3.2 0.7 copy-start.4
  3.9 0.7 copy-start.5
  66.1 1.0 %copy-start.2 = (bf16[384,1536]{1,0:T(8,128)(2,1)}, bf16[384,1536]{1,0:T(8,128)(2,1)S(1)}, u32[]{:S(2)}) copy-start(bf16[384,1536]{1,0:T(8,128)(2,1)S(1)} %get-tuple-element.10.refs_2_) | copy-start | bytes 3538948
  67.2 1.0 %copy-start.3 = (bf16[1536,384]{1,0:T(8,128)(2,1)}, bf16[1536,384]{1,0:T(8,128)(2,1)S(1)}, u32[]{:S(2)}) copy-start(bf16[1536,384]{1,0:T(8,128)(2,1)S(1)} %get-tuple-element.11.refs_3_) | copy-start | bytes 3538948
  68.2 0.6 copy-start.6
  68.8 0.6 copy-start.7

commit v2 on v1

--- a/solution.py
+++ b/solution.py
@@ -16,20 +16,45 @@
 DEPTH = 384
 UNITS = 1536
 HALF = 768
-
-PARENT = {
+PIECES = 4
+VMEM_LIMIT = 58 * 1024 * 1024
+
+SUM_PARENT = {
     3: 0, -3: 0, 1: 0, -1: 0, 6: 3, -6: -3, 4: 3, -4: -3, 2: 1, -2: -1, 8: 6, 7: 6, -7: -6, 5: 4, -5: -4,
 }
-CHILDREN = {}
-for child, parent in PARENT.items():
-    CHILDREN.setdefault(parent, []).append(child)
+UNIT_PARENT = SUM_PARENT
+
+
+def children_of(parents):
+    children = {}
+    for child, parent in parents.items():
+        children.setdefault(parent, []).append(child)
+    return children
+
+
+SUM_CHILDREN, UNIT_CHILDREN = children_of(SUM_PARENT), children_of(UNIT_PARENT)
+
+
+def height(role):
+    return 1 + max((height(child) for child in SUM_CHILDREN.get(role, ())), default=-1)
+
+
+def depth(role):
+    return 1 + depth(UNIT_PARENT[role]) if role else 0
+
+
+def levels(rank, parents):
+    found = {}
+    for role in sorted(parents, key=lambda role: -abs(role)):
+        found.setdefault(rank(role), []).append(role)
+    return [found[level] for level in sorted(found)]
+
+
+SUM_LEVELS, UNIT_LEVELS = levels(height, SUM_PARENT), levels(depth, UNIT_PARENT)
 FAR_FIRST = (
     (2, 2), (1, 2), (3, 2), (2, 1), (2, 3), (0, 2), (2, 0), (1, 1), (1, 3), (3, 1), (3, 3), (0, 1), (0, 3), (1, 0), (3, 0),
 )
-FIRST = (8, 7, -7, 5, -5, 2, -2)
-SECOND = (6, -6, 4, -4, 1, -1)
-THIRD = (3, -3)
-OFFSETS = sorted({PARENT[r] - r for r in PARENT} | {r - PARENT[r] for r in PARENT})
+OFFSETS = sorted({way * (tree[r] - r) for tree in (SUM_PARENT, UNIT_PARENT) for r in tree for way in (1, -1)})
 MIDDLE, LOW, HIGH = range(4, 12), range(0, 4), range(12, 16)
 
 
@@ -53,6 +78,7 @@
     inputs, w_in, w_out, cotangent,
     output, input_grad, w_in_grad, w_out_grad,
     tokens, tokens_twin, w_in_v, w_out_v, w_in_twin, w_out_twin, mine, sums, sums_in, units, send_out, recv_out,
+    grad_in, grad_out, result, store_sem,
     load_sem, own_sem, gather_send, gather_recv, pair_send, pair_recv, swap_send, swap_recv, sum_send, sum_recv,
     unit_send, unit_recv, twin_send, twin_recv, out_send, out_recv,
 ):
@@ -120,12 +146,12 @@
             wait(w_out_twin, swap_recv.at[1])
             wait(tokens_twin.at[1], pair_recv.at[1])
             mine[1] += contract_last(tokens_twin[1], w_out_twin[...])
-        for role in FIRST:
+        for role in SUM_LEVELS[0]:
             pass_on(k, role)
 
     def collected(k, role):
         value = mine[k, rows(role)]
-        for child in CHILDREN.get(role, ()):
+        for child in SUM_CHILDREN.get(role, ()):
             wait(sums_in.at[k, rows(child)], sum_recv.at[k, child + 7])
             value = value + sums_in[k, rows(child)].astype(jnp.float32)
         return value
@@ -134,11 +160,11 @@
         sums[k, rows(role)] = collected(k, role).astype(jnp.bfloat16)
         send(
             sums.at[k, rows(role)], sums_in.at[k, rows(role)], sum_send.at[k], sum_recv.at[k, role + 7],
-            along(PARENT[role] - role),
+            along(SUM_PARENT[role] - role),
         )
 
     def hand_out(k, role):
-        for child in CHILDREN.get(role, ()):
+        for child in UNIT_CHILDREN.get(role, ()):
             send(
                 units.at[k, c, rows(role)], units.at[k, c, rows(child)], unit_send.at[k], unit_recv.at[k, child + 7],
                 along(child - role),
@@ -174,12 +200,10 @@
 
     first_round(0)
     first_round(1)
-    for k in range(2):
-        for role in SECOND:
-            pass_on(k, role)
-    for k in range(2):
-        for role in THIRD:
-            pass_on(k, role)
+    for level in SUM_LEVELS[1:]:
+        for k in range(2):
+            for role in level:
+                pass_on(k, role)
 
     pre_act = collected(0, 0)
     inner = jnp.tanh(gelu_coef * (pre_act + cubic_coef * pre_act * pre_act * pre_act))
@@ -191,27 +215,34 @@
     units[1, c, rows(0)] = (collected(1, 0) * slope).astype(jnp.bfloat16)
     hand_out(1, 0)
 
-    for group in (THIRD + (1, -1), (6, -6, 4, -4, 2, -2)):
+    for level in UNIT_LEVELS[:-1]:
         for k in range(2):
-            for role in group:
+            for role in level:
                 relay(k, role)
     for k in range(2):
         unit_terms(k, 0, MIDDLE)
-        for role in (8, 7, -7, 5, -5):
+        for role in UNIT_LEVELS[-1]:
             relay(k, role)
     for k in range(2):
         unit_terms(k, 1, LOW)
         unit_terms(k, 2, HIGH)
+    stores = []
     for h in range(2):
         span = pl.ds(h * HALF, HALF)
-        w_out_grad[span, :] = contract_first(units[0, h], tokens[1]).astype(jnp.bfloat16)
-        w_in_grad[:, span] = contract_first(tokens[0], units[1, h]).astype(jnp.bfloat16)
+        grad_out[h] = contract_first(units[0, h], tokens[1]).astype(jnp.bfloat16)
+        grad_in[h] = contract_first(tokens[0], units[1, h]).astype(jnp.bfloat16)
+        stores.append(pltpu.make_async_copy(grad_out.at[h], w_out_grad.at[span], store_sem.at[h]))
+        stores.append(pltpu.make_async_copy(grad_in.at[h], w_in_grad.at[:, span], store_sem.at[2 + h]))
+        stores[-2].start()
+        stores[-1].start()
     for k in range(2):
         wait(recv_out.at[k, pl.ds(0, COLS - 1)], out_recv.at[k])
         value = recv_out[k, 0].astype(jnp.float32)
         for source in range(1, COLS):
             value = value + recv_out[k, source].astype(jnp.float32)
-        (output, input_grad)[k][...] = value.astype(jnp.bfloat16)
+        result[k] = value.astype(jnp.bfloat16)
+        stores.append(pltpu.make_async_copy(result.at[k], (output, input_grad)[k], store_sem.at[4 + k]))
+        stores[-1].start()
 
     for k in range(2):
         span = pl.ds(0, (COLS - 1) * BLOCK)
@@ -223,10 +254,17 @@
         wait(send_out.at[k, span], out_send.at[k])
     wait(w_in_twin, swap_send.at[0])
     wait(w_out_twin, swap_send.at[1])
+    for copy in stores:
+        copy.wait()
 
 
 def place(*refs):
-    copies = [pltpu.make_async_copy(refs[i], refs[4 + i], refs[8].at[i]) for i in range(4)]
+    pairs = list(zip(refs[:2], refs[4:6]))
+    for source, target in zip(refs[2:4], refs[6:8]):
+        count = source.shape[0] // PIECES
+        spans = [pl.ds(i * count, count) for i in range(PIECES)]
+        pairs += [(source.at[span], target.at[span]) for span in spans]
+    copies = [pltpu.make_async_copy(source, target, refs[8].at[i]) for i, (source, target) in enumerate(pairs)]
     for copy in copies:
         copy.start()
     for copy in copies:
@@ -236,7 +274,7 @@
 def exchange(inputs, w_in, w_out, cotangent):
     bf16, f32 = jnp.bfloat16, jnp.float32
     dma = pltpu.SemaphoreType.DMA
-    hbm, vmem = pl.BlockSpec(memory_space=pltpu.HBM), pl.BlockSpec(memory_space=pltpu.VMEM)
+    hbm = pl.BlockSpec(memory_space=pltpu.HBM)
     shape = jax.ShapeDtypeStruct
     return pl.pallas_call(
         kernel,
@@ -247,7 +285,7 @@
             shape((UNITS, DEPTH), bf16),
         ),
         in_specs=[hbm] * 4,
-        out_specs=(vmem,) * 4,
+        out_specs=(hbm,) * 4,
         scratch_shapes=[
             pltpu.VMEM((2, TOKENS, DEPTH), bf16),
             pltpu.VMEM((2, TOKENS, DEPTH), bf16),
@@ -261,11 +299,15 @@
             pltpu.VMEM((2, 2, TOKENS, HALF), bf16),
             pltpu.VMEM((2, TOKENS, DEPTH), bf16),
             pltpu.VMEM((2, COLS, BLOCK, DEPTH), bf16),
+            pltpu.VMEM((2, DEPTH, HALF), bf16),
+            pltpu.VMEM((2, HALF, DEPTH), bf16),
+            pltpu.VMEM((2, BLOCK, DEPTH), bf16),
+            dma((6,)),
             dma((4,)), dma((2,)), dma((2,)), dma((2,)), dma((2,)), dma((2,)), dma((2,)), dma((2,)),
             dma((2,)), dma((2, 16)), dma((2,)), dma((2, 16)), dma((2,)), dma((2, 3)), dma((2,)), dma((2,)),
         ],
         compiler_params=pltpu.CompilerParams(
-            collective_id=0, has_side_effects=True, vmem_limit_bytes=40 * 1024 * 1024
+            collective_id=0, has_side_effects=True, vmem_limit_bytes=VMEM_LIMIT
         ),
         name="feed_forward",
     )(inputs, w_in, w_out, cotangent)
@@ -276,9 +318,10 @@
     return pl.pallas_call(
         place,
         out_shape=tuple(jax.ShapeDtypeStruct(result.shape, result.dtype) for result in results),
-        in_specs=[pl.BlockSpec(memory_space=pltpu.VMEM)] * 4,
+        in_specs=[pl.BlockSpec(memory_space=pltpu.HBM)] * 4,
         out_specs=(pl.BlockSpec(memory_space=pltpu.HBM),) * 4,
-        scratch_shapes=[pltpu.SemaphoreType.DMA((4,))],
+        scratch_shapes=[pltpu.SemaphoreType.DMA((2 + 2 * PIECES,))],
+        compiler_params=pltpu.CompilerParams(vmem_limit_bytes=VMEM_LIMIT),
         name="place",
     )(*results)
 

time: 72.8 us -> 136 us (1.87)
  the two profiles are of different devices: /device:TPU:4 before, /device:TPU:2 now
where the time goes in v2:
time: 136 us
  Pallas kernels  135 us (99%)
    pallas_call x1, Pallas kernels, local(): pl.pallas_call(place, out_shape=tuple((jax.ShapeDtypeStruct(result.shape,...  73.4 us
    pallas_call x1, Pallas kernels, exchange(): pl.pallas_call(kernel, out_shape=(shape((BLOCK, DEPTH), bf16), shape((BLO...  61.6 us

profile of v2, /device:TPU:2, one launch (start us, length us, event | category | flops | bytes accessed | tf_op | source)
XLA Modules:
  0.0 135.7 jit_solution(12403400333386580272)
XLA Ops:
  0.6 61.6 %feed_forward.1 = (bf16[16,384]{1,0:T(8,128)(2,1)}, bf16[16,384]{1,0:T(8,128)(2,1)}, bf16[384,1536]{1,0:T(8,128)(2,1)}, bf16[1536,384]{1,0:T(8,128)(2,1)}) custom-call(bf16[16,384]{1,0:T(8,128)(2,1)} %inputs.1, bf16[384,1536]{1,0:T(8,128)(2,1)} %w_in.1, bf16[1536,384]{1,0:T(8,128)(2,1)} %w_out.1, bf16[16,384]{1,0:T(8,128)(2,1)} %cotangent.1), custom_call_target="tpu_custom_call" | custom-call | tf_op jit(solution)/shard_map/feed_forward/pallas_call | solution.py:279
  62.3 73.4 %place.1 = (bf16[16,384]{1,0:T(8,128)(2,1)}, bf16[16,384]{1,0:T(8,128)(2,1)}, bf16[384,1536]{1,0:T(8,128)(2,1)}, bf16[1536,384]{1,0:T(8,128)(2,1)}) custom-call(bf16[16,384]{1,0:T(8,128)(2,1)} %get-tuple-element.8.refs_0_, bf16[16,384]{1,0:T(8,128)(2,1)} %get-tuple-element.9.refs_1_, bf16[384,1536]{1,0:T(8,128)(2,1)} %get-tuple-element.10.refs_2_, ...), custom_call_target="tpu_custom_call" | custom-call | tf_op jit(solution)/shard_map/place/pallas_call | solution.py:318

commit v3 on v2

--- a/solution.py
+++ b/solution.py
@@ -19,42 +19,41 @@
 PIECES = 4
 VMEM_LIMIT = 58 * 1024 * 1024
 
-SUM_PARENT = {
-    3: 0, -3: 0, 1: 0, -1: 0, 6: 3, -6: -3, 4: 3, -4: -3, 2: 1, -2: -1, 8: 6, 7: 6, -7: -6, 5: 4, -5: -4,
+SIDES = {
+    3: 0, -3: 0, 1: 0, -1: 0, 6: 3, -6: -3, 4: 3, -4: -3, 2: 1, -2: -1, 7: 6, -7: -6, 5: 4, -5: -4,
 }
-UNIT_PARENT = SUM_PARENT
+PARENTS = (SIDES | {8: 6}, SIDES | {8: -6})
 
 
 def children_of(parents):
     children = {}
-    for child, parent in parents.items():
-        children.setdefault(parent, []).append(child)
+    for child in sorted(parents, key=lambda role: -abs(role)):
+        children.setdefault(parents[child], []).append(child)
     return children
 
 
-SUM_CHILDREN, UNIT_CHILDREN = children_of(SUM_PARENT), children_of(UNIT_PARENT)
-
-
-def height(role):
-    return 1 + max((height(child) for child in SUM_CHILDREN.get(role, ())), default=-1)
-
-
-def depth(role):
-    return 1 + depth(UNIT_PARENT[role]) if role else 0
-
-
-def levels(rank, parents):
+def depth(role, parents):
+    return 1 + depth(parents[role], parents) if role else 0
+
+
+def height(role, children):
+    return 1 + max((height(child, children) for child in children.get(role, ())), default=-1)
+
+
+def levels(rank, parents, tree):
     found = {}
     for role in sorted(parents, key=lambda role: -abs(role)):
-        found.setdefault(rank(role), []).append(role)
+        found.setdefault(rank(role, tree), []).append(role)
     return [found[level] for level in sorted(found)]
 
 
-SUM_LEVELS, UNIT_LEVELS = levels(height, SUM_PARENT), levels(depth, UNIT_PARENT)
+CHILDREN = [children_of(parents) for parents in PARENTS]
+SUM_LEVELS = [levels(height, parents, children) for parents, children in zip(PARENTS, CHILDREN)]
+UNIT_LEVELS = [levels(depth, parents, parents) for parents in PARENTS]
 FAR_FIRST = (
     (2, 2), (1, 2), (3, 2), (2, 1), (2, 3), (0, 2), (2, 0), (1, 1), (1, 3), (3, 1), (3, 3), (0, 1), (0, 3), (1, 0), (3, 0),
 )
-OFFSETS = sorted({way * (tree[r] - r) for tree in (SUM_PARENT, UNIT_PARENT) for r in tree for way in (1, -1)})
+OFFSETS = sorted({(way * (tree[r] - r) + 8) % CHIPS - 8 for tree in PARENTS for r in tree for way in (1, -1)})
 MIDDLE, LOW, HIGH = range(4, 12), range(0, 4), range(12, 16)
 
 
@@ -146,12 +145,12 @@
             wait(w_out_twin, swap_recv.at[1])
             wait(tokens_twin.at[1], pair_recv.at[1])
             mine[1] += contract_last(tokens_twin[1], w_out_twin[...])
-        for role in SUM_LEVELS[0]:
+        for role in SUM_LEVELS[k][0]:
             pass_on(k, role)
 
     def collected(k, role):
         value = mine[k, rows(role)]
-        for child in SUM_CHILDREN.get(role, ()):
+        for child in CHILDREN[k].get(role, ()):
             wait(sums_in.at[k, rows(child)], sum_recv.at[k, child + 7])
             value = value + sums_in[k, rows(child)].astype(jnp.float32)
         return value
@@ -160,21 +159,26 @@
         sums[k, rows(role)] = collected(k, role).astype(jnp.bfloat16)
         send(
             sums.at[k, rows(role)], sums_in.at[k, rows(role)], sum_send.at[k], sum_recv.at[k, role + 7],
-            along(SUM_PARENT[role] - role),
+            along(PARENTS[k][role] - role),
         )
 
     def hand_out(k, role):
-        for child in UNIT_CHILDREN.get(role, ()):
+        for child in CHILDREN[k].get(role, ()):
             send(
                 units.at[k, c, rows(role)], units.at[k, c, rows(child)], unit_send.at[k], unit_recv.at[k, child + 7],
                 along(child - role),
             )
+
+    def hand_over(k, role):
         group = 0 if role + 7 in MIDDLE else 1 if role + 7 in LOW else 2
         send(units.at[k, c, rows(role)], units.at[k, c, rows(role)], twin_send.at[k], twin_recv.at[k, group], twin)
 
-    def relay(k, role):
-        wait(units.at[k, c, rows(role)], unit_recv.at[k, role + 7])
-        hand_out(k, role)
+    def relay(k, roles):
+        for role in roles:
+            wait(units.at[k, c, rows(role)], unit_recv.at[k, role + 7])
+            hand_out(k, role)
+        for role in roles:
+            hand_over(k, role)
 
     def unit_terms(k, group, blocks):
         span = pl.ds(blocks[0] * BLOCK, len(blocks) * BLOCK)
@@ -200,29 +204,29 @@
 
     first_round(0)
     first_round(1)
-    for level in SUM_LEVELS[1:]:
+    for level in range(1, 3):
         for k in range(2):
-            for role in level:
+            for role in SUM_LEVELS[k][level]:
                 pass_on(k, role)
 
     pre_act = collected(0, 0)
     inner = jnp.tanh(gelu_coef * (pre_act + cubic_coef * pre_act * pre_act * pre_act))
     units[0, c, rows(0)] = (0.5 * pre_act * (1.0 + inner)).astype(jnp.bfloat16)
     hand_out(0, 0)
+    hand_over(0, 0)
     slope = 0.5 * (1.0 + inner) + 0.5 * pre_act * (1.0 - inner * inner) * gelu_coef * (
         1.0 + 3.0 * cubic_coef * pre_act * pre_act
     )
     units[1, c, rows(0)] = (collected(1, 0) * slope).astype(jnp.bfloat16)
     hand_out(1, 0)
-
-    for level in UNIT_LEVELS[:-1]:
+    hand_over(1, 0)
+
+    for level in range(2):
         for k in range(2):
-            for role in level:
-                relay(k, role)
+            relay(k, UNIT_LEVELS[k][level])
     for k in range(2):
         unit_terms(k, 0, MIDDLE)
-        for role in UNIT_LEVELS[-1]:
-            relay(k, role)
+        relay(k, UNIT_LEVELS[k][2])
     for k in range(2):
         unit_terms(k, 1, LOW)
         unit_terms(k, 2, HIGH)
@@ -259,15 +263,19 @@
 
 
 def place(*refs):
-    pairs = list(zip(refs[:2], refs[4:6]))
-    for source, target in zip(refs[2:4], refs[6:8]):
+    pairs = list(zip(refs[:2], refs[8:10], refs[4:6]))
+    for source, middle, target in zip(refs[2:4], refs[10:12], refs[6:8]):
         count = source.shape[0] // PIECES
         spans = [pl.ds(i * count, count) for i in range(PIECES)]
-        pairs += [(source.at[span], target.at[span]) for span in spans]
-    copies = [pltpu.make_async_copy(source, target, refs[8].at[i]) for i, (source, target) in enumerate(pairs)]
-    for copy in copies:
+        pairs += [(source.at[span], middle.at[span], target.at[span]) for span in spans]
+    reads = [pltpu.make_async_copy(pair[0], pair[1], refs[12].at[i]) for i, pair in enumerate(pairs)]
+    writes = [pltpu.make_async_copy(pair[1], pair[2], refs[13].at[i]) for i, pair in enumerate(pairs)]
+    for copy in reads:
         copy.start()
-    for copy in copies:
+    for read, write in zip(reads, writes):
+        read.wait()
+        write.start()
+    for copy in writes:
         copy.wait()
 
 
@@ -320,7 +328,8 @@
         out_shape=tuple(jax.ShapeDtypeStruct(result.shape, result.dtype) for result in results),
         in_specs=[pl.BlockSpec(memory_space=pltpu.HBM)] * 4,
         out_specs=(pl.BlockSpec(memory_space=pltpu.HBM),) * 4,
-        scratch_shapes=[pltpu.SemaphoreType.DMA((2 + 2 * PIECES,))],
+        scratch_shapes=[pltpu.VMEM(result.shape, result.dtype) for result in results]
+        + [pltpu.SemaphoreType.DMA((2 + 2 * PIECES,))] * 2,
         compiler_params=pltpu.CompilerParams(vmem_limit_bytes=VMEM_LIMIT),
         name="place",
     )(*results)

time: 136 us -> 64.1 us (0.47)
  the two profiles are of different devices: /device:TPU:2 before, /device:TPU:4 now
where the time goes in v3:
time: 64.1 us; the launch traced here: 63.9 us
  Pallas kernels  63.3 us (99%)
    pallas_call x1, Pallas kernels, exchange(): pl.pallas_call(kernel, out_shape=(shape((BLOCK, DEPTH), bf16), shape((BLO...  60.7 us
    pallas_call x1, Pallas kernels, local(): pl.pallas_call(place, out_shape=tuple((jax.ShapeDtypeStruct(result.shape,...  2.56 us

profile of v3, /device:TPU:4, one launch (start us, length us, event | category | flops | bytes accessed | tf_op | source)
XLA Modules:
  0.0 63.9 jit_solution(10224567489459721935)
XLA Ops:
  0.6 60.7 %feed_forward.1 = (bf16[16,384]{1,0:T(8,128)(2,1)}, bf16[16,384]{1,0:T(8,128)(2,1)}, bf16[384,1536]{1,0:T(8,128)(2,1)}, bf16[1536,384]{1,0:T(8,128)(2,1)}) custom-call(bf16[16,384]{1,0:T(8,128)(2,1)} %inputs.1, bf16[384,1536]{1,0:T(8,128)(2,1)} %w_in.1, bf16[1536,384]{1,0:T(8,128)(2,1)} %w_out.1, bf16[16,384]{1,0:T(8,128)(2,1)} %cotangent.1), custom_call_target="tpu_custom_call" | custom-call | tf_op jit(solution)/shard_map/feed_forward/pallas_call | solution.py:287
  61.4 2.6 %place.1 = (bf16[16,384]{1,0:T(8,128)(2,1)}, bf16[16,384]{1,0:T(8,128)(2,1)}, bf16[384,1536]{1,0:T(8,128)(2,1)}, bf16[1536,384]{1,0:T(8,128)(2,1)}) custom-call(bf16[16,384]{1,0:T(8,128)(2,1)} %get-tuple-element.8.refs_0_, bf16[16,384]{1,0:T(8,128)(2,1)} %get-tuple-element.9.refs_1_, bf16[384,1536]{1,0:T(8,128)(2,1)} %get-tuple-element.10.refs_2_, ...), custom_call_target="tpu_custom_call" | custom-call | tf_op jit(solution)/shard_map/place/pallas_call | solution.py:326

commit v4 on v3

--- a/solution.py
+++ b/solution.py
@@ -17,7 +17,7 @@
 UNITS = 1536
 HALF = 768
 PIECES = 4
-VMEM_LIMIT = 58 * 1024 * 1024
+VMEM_LIMIT = 32 * 1024 * 1024
 
 SIDES = {
     3: 0, -3: 0, 1: 0, -1: 0, 6: 3, -6: -3, 4: 3, -4: -3, 2: 1, -2: -1, 7: 6, -7: -6, 5: 4, -5: -4,
@@ -54,11 +54,16 @@
     (2, 2), (1, 2), (3, 2), (2, 1), (2, 3), (0, 2), (2, 0), (1, 1), (1, 3), (3, 1), (3, 3), (0, 1), (0, 3), (1, 0), (3, 0),
 )
 OFFSETS = sorted({(way * (tree[r] - r) + 8) % CHIPS - 8 for tree in PARENTS for r in tree for way in (1, -1)})
-MIDDLE, LOW, HIGH = range(4, 12), range(0, 4), range(12, 16)
+SHIFT = 3
+NEAR, FAR = range(0, 8), range(8, 16)
+
+
+def place_of(role):
+    return (role + SHIFT) % CHIPS
 
 
 def rows(role):
-    return pl.ds((role + 7) * BLOCK, BLOCK)
+    return pl.ds(place_of(role) * BLOCK, BLOCK)
 
 
 def contract_last(left, right):
@@ -77,7 +82,6 @@
     inputs, w_in, w_out, cotangent,
     output, input_grad, w_in_grad, w_out_grad,
     tokens, tokens_twin, w_in_v, w_out_v, w_in_twin, w_out_twin, mine, sums, sums_in, units, send_out, recv_out,
-    grad_in, grad_out, result, store_sem,
     load_sem, own_sem, gather_send, gather_recv, pair_send, pair_recv, swap_send, swap_recv, sum_send, sum_recv,
     unit_send, unit_recv, twin_send, twin_recv, out_send, out_recv,
 ):
@@ -100,7 +104,8 @@
     def wait(ref, sem):
         pltpu.make_async_copy(ref, ref, sem).wait()
 
-    here = pl.ds(pl.multiple_of(lax.rem(z - col + 7 + CHIPS, CHIPS) * BLOCK, BLOCK), BLOCK)
+    here_at = lax.rem(z - col + SHIFT + CHIPS, CHIPS)
+    here = pl.ds(pl.multiple_of(here_at * BLOCK, BLOCK), BLOCK)
 
     own = [
         pltpu.make_async_copy(source, tokens.at[k, here], own_sem.at[k])
@@ -114,7 +119,8 @@
         copy.start()
 
     barrier = pltpu.get_barrier_semaphore()
-    peers = [across(step) for step in FAR_FIRST] + [along(offset) for offset in OFFSETS] + [twin]
+    peers = [across(step) for step in FAR_FIRST[:5]] + [along(offset) for offset in OFFSETS]
+    peers += [across(step) for step in FAR_FIRST[5:]] + [twin]
     for peer in peers:
         pl.semaphore_signal(barrier, inc=1, device_id=peer, device_id_type=MESH)
     pl.semaphore_wait(barrier, len(peers))
@@ -132,9 +138,11 @@
     for copy in loads:
         copy.wait()
 
-    def first_round(k):
+    def swap_tokens(k):
         wait(tokens.at[k, pl.ds(0, (COLS - 1) * BLOCK)], gather_recv.at[k])
         send(tokens.at[k], tokens_twin.at[k], pair_send.at[k], pair_recv.at[k], twin)
+
+    def width_terms(k):
         if k == 0:
             mine[0] = jnp.dot(tokens[0], w_in_v[c], preferred_element_type=jnp.float32)
             wait(w_in_twin, swap_recv.at[0])
@@ -145,65 +153,73 @@
             wait(w_out_twin, swap_recv.at[1])
             wait(tokens_twin.at[1], pair_recv.at[1])
             mine[1] += contract_last(tokens_twin[1], w_out_twin[...])
-        for role in SUM_LEVELS[k][0]:
-            pass_on(k, role)
 
     def collected(k, role):
         value = mine[k, rows(role)]
         for child in CHILDREN[k].get(role, ()):
-            wait(sums_in.at[k, rows(child)], sum_recv.at[k, child + 7])
+            wait(sums_in.at[k, rows(child)], sum_recv.at[k, place_of(child)])
             value = value + sums_in[k, rows(child)].astype(jnp.float32)
         return value
 
     def pass_on(k, role):
         sums[k, rows(role)] = collected(k, role).astype(jnp.bfloat16)
         send(
-            sums.at[k, rows(role)], sums_in.at[k, rows(role)], sum_send.at[k], sum_recv.at[k, role + 7],
+            sums.at[k, rows(role)], sums_in.at[k, rows(role)], sum_send.at[k], sum_recv.at[k, place_of(role)],
             along(PARENTS[k][role] - role),
         )
 
     def hand_out(k, role):
         for child in CHILDREN[k].get(role, ()):
             send(
-                units.at[k, c, rows(role)], units.at[k, c, rows(child)], unit_send.at[k], unit_recv.at[k, child + 7],
+                units.at[k, c, rows(role)], units.at[k, c, rows(child)], unit_send.at[k], unit_recv.at[k, place_of(child)],
                 along(child - role),
             )
 
     def hand_over(k, role):
-        group = 0 if role + 7 in MIDDLE else 1 if role + 7 in LOW else 2
+        group = 0 if place_of(role) in NEAR else 1
         send(units.at[k, c, rows(role)], units.at[k, c, rows(role)], twin_send.at[k], twin_recv.at[k, group], twin)
 
     def relay(k, roles):
         for role in roles:
-            wait(units.at[k, c, rows(role)], unit_recv.at[k, role + 7])
+            wait(units.at[k, c, rows(role)], unit_recv.at[k, place_of(role)])
             hand_out(k, role)
         for role in roles:
             hand_over(k, role)
 
-    def unit_terms(k, group, blocks):
+    def unit_terms(k, group):
+        blocks = (NEAR, FAR)[group]
         span = pl.ds(blocks[0] * BLOCK, len(blocks) * BLOCK)
+
+        def terms(h):
+            if k == 0:
+                return jnp.dot(units[0, h, span], w_out_v[h], preferred_element_type=jnp.float32)
+            return contract_last(units[1, h, span], w_in_v[h])
+
+        value = terms(c)
         wait(units.at[k, 1 - c, span], twin_recv.at[k, group])
-        if k == 0:
-            value = jnp.dot(units[0, 0, span], w_out_v[0], preferred_element_type=jnp.float32)
-            value = value + jnp.dot(units[0, 1, span], w_out_v[1], preferred_element_type=jnp.float32)
-        else:
-            value = contract_last(units[1, 0, span], w_in_v[0])
-            value = value + contract_last(units[1, 1, span], w_in_v[1])
+        value = value + terms(1 - c)
         send_out[k, span] = value.astype(jnp.bfloat16)
-        for p in blocks:
-            target = lax.rem(z + 7 - p + CHIPS, CHIPS)
-            source = send_out.at[k, pl.ds(p * BLOCK, BLOCK)]
-
-            @pl.when(target != col)
+        for step in FAR_FIRST:
+            device = across(step)
+            p = lax.rem(z - device[1] + SHIFT + CHIPS, CHIPS)
+
+            @pl.when((p >= blocks[0]) & (p <= blocks[-1]))
             def _():
-                send(source, recv_out.at[k, col], out_send.at[k], out_recv.at[k], (row, target))
-
-            @pl.when(target == col)
-            def _():
-                recv_out[k, col] = source[...]
-
-    first_round(0)
-    first_round(1)
+                block = pl.ds(pl.multiple_of(p * BLOCK, BLOCK), BLOCK)
+                send(send_out.at[k, block], recv_out.at[k, col], out_send.at[k], out_recv.at[k], device)
+
+        @pl.when((here_at >= blocks[0]) & (here_at <= blocks[-1]))
+        def _():
+            recv_out[k, col] = send_out[k, here]
+
+    swap_tokens(0)
+    width_terms(0)
+    swap_tokens(1)
+    for role in SUM_LEVELS[0][0]:
+        pass_on(0, role)
+    width_terms(1)
+    for role in SUM_LEVELS[1][0]:
+        pass_on(1, role)
     for level in range(1, 3):
         for k in range(2):
             for role in SUM_LEVELS[k][level]:
@@ -225,28 +241,20 @@
         for k in range(2):
             relay(k, UNIT_LEVELS[k][level])
     for k in range(2):
-        unit_terms(k, 0, MIDDLE)
+        unit_terms(k, 0)
         relay(k, UNIT_LEVELS[k][2])
     for k in range(2):
-        unit_terms(k, 1, LOW)
-        unit_terms(k, 2, HIGH)
-    stores = []
+        unit_terms(k, 1)
     for h in range(2):
         span = pl.ds(h * HALF, HALF)
-        grad_out[h] = contract_first(units[0, h], tokens[1]).astype(jnp.bfloat16)
-        grad_in[h] = contract_first(tokens[0], units[1, h]).astype(jnp.bfloat16)
-        stores.append(pltpu.make_async_copy(grad_out.at[h], w_out_grad.at[span], store_sem.at[h]))
-        stores.append(pltpu.make_async_copy(grad_in.at[h], w_in_grad.at[:, span], store_sem.at[2 + h]))
-        stores[-2].start()
-        stores[-1].start()
+        w_out_grad[span] = contract_first(units[0, h], tokens[1]).astype(jnp.bfloat16)
+        w_in_grad[:, span] = contract_first(tokens[0], units[1, h]).astype(jnp.bfloat16)
     for k in range(2):
         wait(recv_out.at[k, pl.ds(0, COLS - 1)], out_recv.at[k])
         value = recv_out[k, 0].astype(jnp.float32)
         for source in range(1, COLS):
             value = value + recv_out[k, source].astype(jnp.float32)
-        result[k] = value.astype(jnp.bfloat16)
-        stores.append(pltpu.make_async_copy(result.at[k], (output, input_grad)[k], store_sem.at[4 + k]))
-        stores[-1].start()
+        (output, input_grad)[k][...] = value.astype(jnp.bfloat16)
 
     for k in range(2):
         span = pl.ds(0, (COLS - 1) * BLOCK)
@@ -258,42 +266,35 @@
         wait(send_out.at[k, span], out_send.at[k])
     wait(w_in_twin, swap_send.at[0])
     wait(w_out_twin, swap_send.at[1])
-    for copy in stores:
-        copy.wait()
 
 
 def place(*refs):
-    pairs = list(zip(refs[:2], refs[8:10], refs[4:6]))
-    for source, middle, target in zip(refs[2:4], refs[10:12], refs[6:8]):
+    pairs = list(zip(refs[:2], refs[4:6]))
+    for source, target in zip(refs[2:4], refs[6:8]):
         count = source.shape[0] // PIECES
         spans = [pl.ds(i * count, count) for i in range(PIECES)]
-        pairs += [(source.at[span], middle.at[span], target.at[span]) for span in spans]
-    reads = [pltpu.make_async_copy(pair[0], pair[1], refs[12].at[i]) for i, pair in enumerate(pairs)]
-    writes = [pltpu.make_async_copy(pair[1], pair[2], refs[13].at[i]) for i, pair in enumerate(pairs)]
-    for copy in reads:
+        pairs += [(source.at[span], target.at[span]) for span in spans]
+    copies = [pltpu.make_async_copy(source, target, refs[8].at[i]) for i, (source, target) in enumerate(pairs)]
+    for copy in copies:
         copy.start()
-    for read, write in zip(reads, writes):
-        read.wait()
-        write.start()
-    for copy in writes:
+    for copy in copies:
         copy.wait()
 
 
 def exchange(inputs, w_in, w_out, cotangent):
     bf16, f32 = jnp.bfloat16, jnp.float32
     dma = pltpu.SemaphoreType.DMA
-    hbm = pl.BlockSpec(memory_space=pltpu.HBM)
-    shape = jax.ShapeDtypeStruct
+    hbm, vmem = pl.BlockSpec(memory_space=pltpu.HBM), pl.BlockSpec(memory_space=pltpu.VMEM)
     return pl.pallas_call(
         kernel,
         out_shape=(
-            shape((BLOCK, DEPTH), bf16),
-            shape((BLOCK, DEPTH), bf16),
-            shape((DEPTH, UNITS), bf16),
-            shape((UNITS, DEPTH), bf16),
+            pltpu.VMEM((BLOCK, DEPTH), bf16),
+            pltpu.VMEM((BLOCK, DEPTH), bf16),
+            pltpu.VMEM((DEPTH, UNITS), bf16),
+            pltpu.VMEM((UNITS, DEPTH), bf16),
         ),
         in_specs=[hbm] * 4,
-        out_specs=(hbm,) * 4,
+        out_specs=(vmem,) * 4,
         scratch_shapes=[
             pltpu.VMEM((2, TOKENS, DEPTH), bf16),
             pltpu.VMEM((2, TOKENS, DEPTH), bf16),
@@ -307,12 +308,8 @@
             pltpu.VMEM((2, 2, TOKENS, HALF), bf16),
             pltpu.VMEM((2, TOKENS, DEPTH), bf16),
             pltpu.VMEM((2, COLS, BLOCK, DEPTH), bf16),
-            pltpu.VMEM((2, DEPTH, HALF), bf16),
-            pltpu.VMEM((2, HALF, DEPTH), bf16),
-            pltpu.VMEM((2, BLOCK, DEPTH), bf16),
-            dma((6,)),
             dma((4,)), dma((2,)), dma((2,)), dma((2,)), dma((2,)), dma((2,)), dma((2,)), dma((2,)),
-            dma((2,)), dma((2, 16)), dma((2,)), dma((2, 16)), dma((2,)), dma((2, 3)), dma((2,)), dma((2,)),
+            dma((2,)), dma((2, 16)), dma((2,)), dma((2, 16)), dma((2,)), dma((2, 2)), dma((2,)), dma((2,)),
         ],
         compiler_params=pltpu.CompilerParams(
             collective_id=0, has_side_effects=True, vmem_limit_bytes=VMEM_LIMIT
@@ -322,15 +319,15 @@
 
 
 def local(inputs, w_in, w_out, cotangent):
-    results = exchange(inputs, w_in, w_out, cotangent)
+    held = [pltpu.with_memory_space_constraint(array, pltpu.HBM) for array in (inputs, w_in, w_out, cotangent)]
+    results = [pltpu.with_memory_space_constraint(array, pltpu.VMEM) for array in exchange(*held)]
     return pl.pallas_call(
         place,
-        out_shape=tuple(jax.ShapeDtypeStruct(result.shape, result.dtype) for result in results),
-        in_specs=[pl.BlockSpec(memory_space=pltpu.HBM)] * 4,
+        out_shape=tuple(pltpu.HBM(result.shape, result.dtype) for result in results),
+        in_specs=[pl.BlockSpec(memory_space=pltpu.VMEM)] * 4,
         out_specs=(pl.BlockSpec(memory_space=pltpu.HBM),) * 4,
-        scratch_shapes=[pltpu.VMEM(result.shape, result.dtype) for result in results]
-        + [pltpu.SemaphoreType.DMA((2 + 2 * PIECES,))] * 2,
-        compiler_params=pltpu.CompilerParams(vmem_limit_bytes=VMEM_LIMIT),
+        scratch_shapes=[pltpu.SemaphoreType.DMA((2 + 2 * PIECES,))],
+        compiler_params=pltpu.CompilerParams(vmem_limit_bytes=1024 * 1024),
         name="place",
     )(*results)
 

time: 64.1 us -> 62.7 us (0.978)
  the two profiles are of different devices: /device:TPU:4 before, /device:TPU:2 now
where the time goes in v4:
time: 62.7 us; the launch traced here: 62.6 us
  Pallas kernels  62 us (99%)
  between operations  0.64 us (1%)
    pallas_call x1, Pallas kernels, exchange(): pl.pallas_call(kernel, out_shape=(pltpu.VMEM((BLOCK, DEPTH), bf16), pltpu...  60.5 us
    pallas_call x1, Pallas kernels, local(): pl.pallas_call(place, out_shape=tuple((pltpu.HBM(result.shape, result.dty...  1.49 us

profile of v4, /device:TPU:2, one launch (start us, length us, event | category | flops | bytes accessed | tf_op | source)
XLA Modules:
  0.0 62.6 jit_solution(1582016620363043816)
XLA Ops:
  0.6 60.5 %feed_forward.1 = (bf16[16,384]{1,0:T(8,128)(2,1)S(1)}, bf16[16,384]{1,0:T(8,128)(2,1)S(1)}, bf16[384,1536]{1,0:T(8,128)(2,1)S(1)}, bf16[1536,384]{1,0:T(8,128)(2,1)S(1)}) custom-call(bf16[16,384]{1,0:T(8,128)(2,1)} %inputs.1, bf16[384,1536]{1,0:T(8,128)(2,1)} %w_in.1, bf16[1536,384]{1,0:T(8,128)(2,1)} %w_out.1, bf16[16,384]{1,0:T(8,128)(2,1)} %cotangent.1), custom_call_target="tpu_custom_call" | custom-call | tf_op jit(solution)/shard_map/feed_forward/pallas_call | solution.py:288
  61.1 1.5 %place.1 = (bf16[16,384]{1,0:T(8,128)(2,1)}, bf16[16,384]{1,0:T(8,128)(2,1)}, bf16[384,1536]{1,0:T(8,128)(2,1)}, bf16[1536,384]{1,0:T(8,128)(2,1)}) custom-call(bf16[16,384]{1,0:T(8,128)(2,1)S(1)} %get-tuple-element.8.refs_0_, bf16[16,384]{1,0:T(8,128)(2,1)S(1)} %get-tuple-element.9.refs_1_, bf16[384,1536]{1,0:T(8,128)(2,1)S(1)} %get-tuple-element.10.refs_2_, ...), custom_call_target="tpu_custom_call" | custom-call | tf_op jit(solution)/shard_map/place/pallas_call | solution.py:324

commit v5 on v4

--- a/solution.py
+++ b/solution.py
@@ -17,6 +17,8 @@
 UNITS = 1536
 HALF = 768
 PIECES = 4
+PARTS = 2
+WIDE = HALF // PARTS
 VMEM_LIMIT = 32 * 1024 * 1024
 
 SIDES = {
@@ -56,6 +58,10 @@
 OFFSETS = sorted({(way * (tree[r] - r) + 8) % CHIPS - 8 for tree in PARENTS for r in tree for way in (1, -1)})
 SHIFT = 3
 NEAR, FAR = range(0, 8), range(8, 16)
+
+
+def columns(q):
+    return pl.ds(q * WIDE, WIDE)
 
 
 def place_of(role):
@@ -143,48 +149,58 @@
         send(tokens.at[k], tokens_twin.at[k], pair_send.at[k], pair_recv.at[k], twin)
 
     def width_terms(k):
-        if k == 0:
-            mine[0] = jnp.dot(tokens[0], w_in_v[c], preferred_element_type=jnp.float32)
-            wait(w_in_twin, swap_recv.at[0])
-            wait(tokens_twin.at[0], pair_recv.at[0])
-            mine[0] += jnp.dot(tokens_twin[0], w_in_twin[...], preferred_element_type=jnp.float32)
-        else:
-            mine[1] = contract_last(tokens[1], w_out_v[c])
-            wait(w_out_twin, swap_recv.at[1])
-            wait(tokens_twin.at[1], pair_recv.at[1])
-            mine[1] += contract_last(tokens_twin[1], w_out_twin[...])
-
-    def collected(k, role):
-        value = mine[k, rows(role)]
+        for q in range(PARTS):
+            if k == 0:
+                mine[0, :, columns(q)] = jnp.dot(
+                    tokens[0], w_in_v[c, :, columns(q)], preferred_element_type=jnp.float32
+                )
+            else:
+                mine[1, :, columns(q)] = contract_last(tokens[1], w_out_v[c, columns(q)])
+        wait((w_in_twin, w_out_twin)[k], swap_recv.at[k])
+        wait(tokens_twin.at[k], pair_recv.at[k])
+        for q in range(PARTS):
+            if k == 0:
+                mine[0, :, columns(q)] += jnp.dot(
+                    tokens_twin[0], w_in_twin[:, columns(q)], preferred_element_type=jnp.float32
+                )
+            else:
+                mine[1, :, columns(q)] += contract_last(tokens_twin[1], w_out_twin[columns(q)])
+            for role in SUM_LEVELS[k][0]:
+                pass_on(k, q, role)
+
+    def collected(k, q, role):
+        value = mine[k, rows(role), columns(q)]
         for child in CHILDREN[k].get(role, ()):
-            wait(sums_in.at[k, rows(child)], sum_recv.at[k, place_of(child)])
-            value = value + sums_in[k, rows(child)].astype(jnp.float32)
+            wait(sums_in.at[k, rows(child), columns(q)], sum_recv.at[k, q, place_of(child)])
+            value = value + sums_in[k, rows(child), columns(q)].astype(jnp.float32)
         return value
 
-    def pass_on(k, role):
-        sums[k, rows(role)] = collected(k, role).astype(jnp.bfloat16)
+    def pass_on(k, q, role):
+        sums[k, rows(role), columns(q)] = collected(k, q, role).astype(jnp.bfloat16)
         send(
-            sums.at[k, rows(role)], sums_in.at[k, rows(role)], sum_send.at[k], sum_recv.at[k, place_of(role)],
-            along(PARENTS[k][role] - role),
+            sums.at[k, rows(role), columns(q)], sums_in.at[k, rows(role), columns(q)], sum_send.at[k],
+            sum_recv.at[k, q, place_of(role)], along(PARENTS[k][role] - role),
         )
 
-    def hand_out(k, role):
+    def hand_out(k, q, role):
         for child in CHILDREN[k].get(role, ()):
             send(
-                units.at[k, c, rows(role)], units.at[k, c, rows(child)], unit_send.at[k], unit_recv.at[k, place_of(child)],
-                along(child - role),
+                units.at[k, c, rows(role), columns(q)], units.at[k, c, rows(child), columns(q)], unit_send.at[k],
+                unit_recv.at[k, q, place_of(child)], along(child - role),
             )
 
-    def hand_over(k, role):
+    def hand_over(k, q, role):
         group = 0 if place_of(role) in NEAR else 1
-        send(units.at[k, c, rows(role)], units.at[k, c, rows(role)], twin_send.at[k], twin_recv.at[k, group], twin)
+        part = units.at[k, c, rows(role), columns(q)]
+        send(part, part, twin_send.at[k], twin_recv.at[k, group], twin)
 
     def relay(k, roles):
-        for role in roles:
-            wait(units.at[k, c, rows(role)], unit_recv.at[k, place_of(role)])
-            hand_out(k, role)
-        for role in roles:
-            hand_over(k, role)
+        for q in range(PARTS):
+            for role in roles:
+                wait(units.at[k, c, rows(role), columns(q)], unit_recv.at[k, q, place_of(role)])
+                hand_out(k, q, role)
+            for role in roles:
+                hand_over(k, q, role)
 
     def unit_terms(k, group):
         blocks = (NEAR, FAR)[group]
@@ -215,36 +231,38 @@
     swap_tokens(0)
     width_terms(0)
     swap_tokens(1)
-    for role in SUM_LEVELS[0][0]:
-        pass_on(0, role)
     width_terms(1)
-    for role in SUM_LEVELS[1][0]:
-        pass_on(1, role)
     for level in range(1, 3):
         for k in range(2):
-            for role in SUM_LEVELS[k][level]:
-                pass_on(k, role)
-
-    pre_act = collected(0, 0)
-    inner = jnp.tanh(gelu_coef * (pre_act + cubic_coef * pre_act * pre_act * pre_act))
-    units[0, c, rows(0)] = (0.5 * pre_act * (1.0 + inner)).astype(jnp.bfloat16)
-    hand_out(0, 0)
-    hand_over(0, 0)
-    slope = 0.5 * (1.0 + inner) + 0.5 * pre_act * (1.0 - inner * inner) * gelu_coef * (
-        1.0 + 3.0 * cubic_coef * pre_act * pre_act
-    )
-    units[1, c, rows(0)] = (collected(1, 0) * slope).astype(jnp.bfloat16)
-    hand_out(1, 0)
-    hand_over(1, 0)
+            for q in range(PARTS):
+                for role in SUM_LEVELS[k][level]:
+                    pass_on(k, q, role)
+
+    slopes = []
+    for q in range(PARTS):
+        pre_act = collected(0, q, 0)
+        inner = jnp.tanh(gelu_coef * (pre_act + cubic_coef * pre_act * pre_act * pre_act))
+        units[0, c, rows(0), columns(q)] = (0.5 * pre_act * (1.0 + inner)).astype(jnp.bfloat16)
+        hand_out(0, q, 0)
+        hand_over(0, q, 0)
+        slopes.append(
+            0.5 * (1.0 + inner)
+            + 0.5 * pre_act * (1.0 - inner * inner) * gelu_coef * (1.0 + 3.0 * cubic_coef * pre_act * pre_act)
+        )
+    for q in range(PARTS):
+        units[1, c, rows(0), columns(q)] = (collected(1, q, 0) * slopes[q]).astype(jnp.bfloat16)
+        hand_out(1, q, 0)
+        hand_over(1, q, 0)
 
     for level in range(2):
         for k in range(2):
             relay(k, UNIT_LEVELS[k][level])
-    for k in range(2):
-        unit_terms(k, 0)
-        relay(k, UNIT_LEVELS[k][2])
-    for k in range(2):
-        unit_terms(k, 1)
+    unit_terms(0, 0)
+    relay(0, UNIT_LEVELS[0][2])
+    unit_terms(1, 0)
+    unit_terms(0, 1)
+    relay(1, UNIT_LEVELS[1][2])
+    unit_terms(1, 1)
     for h in range(2):
         span = pl.ds(h * HALF, HALF)
         w_out_grad[span] = contract_first(units[0, h], tokens[1]).astype(jnp.bfloat16)
@@ -309,7 +327,7 @@
             pltpu.VMEM((2, TOKENS, DEPTH), bf16),
             pltpu.VMEM((2, COLS, BLOCK, DEPTH), bf16),
             dma((4,)), dma((2,)), dma((2,)), dma((2,)), dma((2,)), dma((2,)), dma((2,)), dma((2,)),
-            dma((2,)), dma((2, 16)), dma((2,)), dma((2, 16)), dma((2,)), dma((2, 2)), dma((2,)), dma((2,)),
+            dma((2,)), dma((2, PARTS, 16)), dma((2,)), dma((2, PARTS, 16)), dma((2,)), dma((2, 2)), dma((2,)), dma((2,)),
         ],
         compiler_params=pltpu.CompilerParams(
             collective_id=0, has_side_effects=True, vmem_limit_bytes=VMEM_LIMIT

time: 62.7 us -> 61.7 us (0.984)
  Pallas kernels: 62 us -> 60.9 us
    pallas_call x1, Pallas kernels: 60.5 us -> 59.4 us  [exchange(): pl.pallas_call(kernel, out_shape=(pltpu.VMEM((BLOCK, DEPTH), bf16), pltpu...]
where the time goes in v5:
time: 61.7 us; the launch traced here: 61.6 us
  Pallas kernels  60.9 us (99%)
  between operations  0.64 us (1%)
    pallas_call x1, Pallas kernels, exchange(): pl.pallas_call(kernel, out_shape=(pltpu.VMEM((BLOCK, DEPTH), bf16), pltpu...  59.4 us
    pallas_call x1, Pallas kernels, local(): pl.pallas_call(place, out_shape=tuple((pltpu.HBM(result.shape, result.dty...  1.49 us

profile of v5, /device:TPU:2, one launch (start us, length us, event | category | flops | bytes accessed | tf_op | source)
XLA Modules:
  0.0 61.6 jit_solution(13724147753432534016)
XLA Ops:
  0.6 59.4 %feed_forward.1 = (bf16[16,384]{1,0:T(8,128)(2,1)S(1)}, bf16[16,384]{1,0:T(8,128)(2,1)S(1)}, bf16[384,1536]{1,0:T(8,128)(2,1)S(1)}, bf16[1536,384]{1,0:T(8,128)(2,1)S(1)}) custom-call(bf16[16,384]{1,0:T(8,128)(2,1)} %inputs.1, bf16[384,1536]{1,0:T(8,128)(2,1)} %w_in.1, bf16[1536,384]{1,0:T(8,128)(2,1)} %w_out.1, bf16[16,384]{1,0:T(8,128)(2,1)} %cotangent.1), custom_call_target="tpu_custom_call" | custom-call | tf_op jit(solution)/shard_map/feed_forward/pallas_call | solution.py:306
  60.1 1.5 %place.1 = (bf16[16,384]{1,0:T(8,128)(2,1)}, bf16[16,384]{1,0:T(8,128)(2,1)}, bf16[384,1536]{1,0:T(8,128)(2,1)}, bf16[1536,384]{1,0:T(8,128)(2,1)}) custom-call(bf16[16,384]{1,0:T(8,128)(2,1)S(1)} %get-tuple-element.8.refs_0_, bf16[16,384]{1,0:T(8,128)(2,1)S(1)} %get-tuple-element.9.refs_1_, bf16[384,1536]{1,0:T(8,128)(2,1)S(1)} %get-tuple-element.10.refs_2_, ...), custom_call_target="tpu_custom_call" | custom-call | tf_op jit(solution)/shard_map/place/pallas_call | solution.py:342

commit v6 on v5

--- a/solution.py
+++ b/solution.py
@@ -38,20 +38,16 @@
     return 1 + depth(parents[role], parents) if role else 0
 
 
-def height(role, children):
-    return 1 + max((height(child, children) for child in children.get(role, ())), default=-1)
-
-
-def levels(rank, parents, tree):
+def levels(parents):
     found = {}
     for role in sorted(parents, key=lambda role: -abs(role)):
-        found.setdefault(rank(role, tree), []).append(role)
+        found.setdefault(depth(role, parents), []).append(role)
     return [found[level] for level in sorted(found)]
 
 
 CHILDREN = [children_of(parents) for parents in PARENTS]
-SUM_LEVELS = [levels(height, parents, children) for parents, children in zip(PARENTS, CHILDREN)]
-UNIT_LEVELS = [levels(depth, parents, parents) for parents in PARENTS]
+UNIT_LEVELS = [levels(parents) for parents in PARENTS]
+SUM_LEVELS = [found[::-1] for found in UNIT_LEVELS]
 FAR_FIRST = (
     (2, 2), (1, 2), (3, 2), (2, 1), (2, 3), (0, 2), (2, 0), (1, 1), (1, 3), (3, 1), (3, 3), (0, 1), (0, 3), (1, 0), (3, 0),
 )

time: 61.7 us -> 61.4 us (level)
  no operation moved by 1% of the time
where the time goes in v6:
time: 61.4 us; the launch traced here: 61.3 us
  Pallas kernels  60.6 us (99%)
  between operations  0.64 us (1%)
    pallas_call x1, Pallas kernels, exchange(): pl.pallas_call(kernel, out_shape=(pltpu.VMEM((BLOCK, DEPTH), bf16), pltpu...  59.1 us
    pallas_call x1, Pallas kernels, local(): pl.pallas_call(place, out_shape=tuple((pltpu.HBM(result.shape, result.dty...  1.49 us

profile of v6, /device:TPU:2, one launch (start us, length us, event | category | flops | bytes accessed | tf_op | source)
XLA Modules:
  0.0 61.3 jit_solution(10811640438453799424)
XLA Ops:
  0.6 59.1 %feed_forward.1 = (bf16[16,384]{1,0:T(8,128)(2,1)S(1)}, bf16[16,384]{1,0:T(8,128)(2,1)S(1)}, bf16[384,1536]{1,0:T(8,128)(2,1)S(1)}, bf16[1536,384]{1,0:T(8,128)(2,1)S(1)}) custom-call(bf16[16,384]{1,0:T(8,128)(2,1)} %inputs.1, bf16[384,1536]{1,0:T(8,128)(2,1)} %w_in.1, bf16[1536,384]{1,0:T(8,128)(2,1)} %w_out.1, bf16[16,384]{1,0:T(8,128)(2,1)} %cotangent.1), custom_call_target="tpu_custom_call" | custom-call | tf_op jit(solution)/shard_map/feed_forward/pallas_call | solution.py:302
  59.8 1.5 %place.1 = (bf16[16,384]{1,0:T(8,128)(2,1)}, bf16[16,384]{1,0:T(8,128)(2,1)}, bf16[384,1536]{1,0:T(8,128)(2,1)}, bf16[1536,384]{1,0:T(8,128)(2,1)}) custom-call(bf16[16,384]{1,0:T(8,128)(2,1)S(1)} %get-tuple-element.8.refs_0_, bf16[16,384]{1,0:T(8,128)(2,1)S(1)} %get-tuple-element.9.refs_1_, bf16[384,1536]{1,0:T(8,128)(2,1)S(1)} %get-tuple-element.10.refs_2_, ...), custom_call_target="tpu_custom_call" | custom-call | tf_op jit(solution)/shard_map/place/pallas_call | solution.py:338

commit v7 on v6

--- a/solution.py
+++ b/solution.py
@@ -46,8 +46,8 @@
 
 
 CHILDREN = [children_of(parents) for parents in PARENTS]
-UNIT_LEVELS = [levels(parents) for parents in PARENTS]
-SUM_LEVELS = [found[::-1] for found in UNIT_LEVELS]
+UNIT_LEVELS = levels(PARENTS[0])
+SUM_LEVELS = UNIT_LEVELS[::-1]
 FAR_FIRST = (
     (2, 2), (1, 2), (3, 2), (2, 1), (2, 3), (0, 2), (2, 0), (1, 1), (1, 3), (3, 1), (3, 3), (0, 1), (0, 3), (1, 0), (3, 0),
 )
@@ -161,12 +161,12 @@
                 )
             else:
                 mine[1, :, columns(q)] += contract_last(tokens_twin[1], w_out_twin[columns(q)])
-            for role in SUM_LEVELS[k][0]:
+            for role in SUM_LEVELS[0]:
                 pass_on(k, q, role)
 
     def collected(k, q, role):
         value = mine[k, rows(role), columns(q)]
-        for child in CHILDREN[k].get(role, ()):
+        for child in CHILDREN[q].get(role, ()):
             wait(sums_in.at[k, rows(child), columns(q)], sum_recv.at[k, q, place_of(child)])
             value = value + sums_in[k, rows(child), columns(q)].astype(jnp.float32)
         return value
@@ -175,11 +175,11 @@
         sums[k, rows(role), columns(q)] = collected(k, q, role).astype(jnp.bfloat16)
         send(
             sums.at[k, rows(role), columns(q)], sums_in.at[k, rows(role), columns(q)], sum_send.at[k],
-            sum_recv.at[k, q, place_of(role)], along(PARENTS[k][role] - role),
+            sum_recv.at[k, q, place_of(role)], along(PARENTS[q][role] - role),
         )
 
     def hand_out(k, q, role):
-        for child in CHILDREN[k].get(role, ()):
+        for child in CHILDREN[q].get(role, ()):
             send(
                 units.at[k, c, rows(role), columns(q)], units.at[k, c, rows(child), columns(q)], unit_send.at[k],
                 unit_recv.at[k, q, place_of(child)], along(child - role),
@@ -231,7 +231,7 @@
     for level in range(1, 3):
         for k in range(2):
             for q in range(PARTS):
-                for role in SUM_LEVELS[k][level]:
+                for role in SUM_LEVELS[level]:
                     pass_on(k, q, role)
 
     slopes = []
@@ -252,18 +252,26 @@
 
     for level in range(2):
         for k in range(2):
-            relay(k, UNIT_LEVELS[k][level])
+            relay(k, UNIT_LEVELS[level])
     unit_terms(0, 0)
-    relay(0, UNIT_LEVELS[0][2])
+    relay(0, UNIT_LEVELS[2])
     unit_terms(1, 0)
     unit_terms(0, 1)
-    relay(1, UNIT_LEVELS[1][2])
+    relay(1, UNIT_LEVELS[2])
     unit_terms(1, 1)
     for h in range(2):
         span = pl.ds(h * HALF, HALF)
         w_out_grad[span] = contract_first(units[0, h], tokens[1]).astype(jnp.bfloat16)
         w_in_grad[:, span] = contract_first(tokens[0], units[1, h]).astype(jnp.bfloat16)
     for k in range(2):
+        span = pl.ds(0, (COLS - 1) * BLOCK)
+        wait(tokens.at[k, span], gather_send.at[k])
+        wait((w_in_twin, w_out_twin)[k], swap_send.at[k])
+        wait(tokens_twin.at[k], pair_send.at[k])
+        wait(sums.at[k, span], sum_send.at[k])
+        wait(units.at[k, 0, span], unit_send.at[k])
+        wait(units.at[k, 0], twin_send.at[k])
+    for k in range(2):
         wait(recv_out.at[k, pl.ds(0, COLS - 1)], out_recv.at[k])
         value = recv_out[k, 0].astype(jnp.float32)
         for source in range(1, COLS):
@@ -271,15 +279,7 @@
         (output, input_grad)[k][...] = value.astype(jnp.bfloat16)
 
     for k in range(2):
-        span = pl.ds(0, (COLS - 1) * BLOCK)
-        wait(tokens.at[k, span], gather_send.at[k])
-        wait(tokens_twin.at[k], pair_send.at[k])
-        wait(sums.at[k, span], sum_send.at[k])
-        wait(units.at[k, 0, span], unit_send.at[k])
-        wait(units.at[k, 0], twin_send.at[k])
-        wait(send_out.at[k, span], out_send.at[k])
-    wait(w_in_twin, swap_send.at[0])
-    wait(w_out_twin, swap_send.at[1])
+        wait(send_out.at[k, pl.ds(0, (COLS - 1) * BLOCK)], out_send.at[k])
 
 
 def place(*refs):

time: 61.4 us -> 60.9 us (level)
  Pallas kernels: 60.6 us -> 59.9 us
    pallas_call x1, Pallas kernels: 59.1 us -> 58.4 us  [exchange(): pl.pallas_call(kernel, out_shape=(pltpu.VMEM((BLOCK, DEPTH), bf16), pltpu...]
where the time goes in v7:
time: 60.9 us; the launch traced here: 60.5 us
  Pallas kernels  59.9 us (98%)
  between operations  0.64 us (1%)
    pallas_call x1, Pallas kernels, exchange(): pl.pallas_call(kernel, out_shape=(pltpu.VMEM((BLOCK, DEPTH), bf16), pltpu...  58.4 us
    pallas_call x1, Pallas kernels, local(): pl.pallas_call(place, out_shape=tuple((pltpu.HBM(result.shape, result.dty...  1.49 us

profile of v7, /device:TPU:2, one launch (start us, length us, event | category | flops | bytes accessed | tf_op | source)
XLA Modules:
  0.0 60.5 jit_solution(7185443708748836)
XLA Ops:
  0.6 58.4 %feed_forward.1 = (bf16[16,384]{1,0:T(8,128)(2,1)S(1)}, bf16[16,384]{1,0:T(8,128)(2,1)S(1)}, bf16[384,1536]{1,0:T(8,128)(2,1)S(1)}, bf16[1536,384]{1,0:T(8,128)(2,1)S(1)}) custom-call(bf16[16,384]{1,0:T(8,128)(2,1)} %inputs.1, bf16[384,1536]{1,0:T(8,128)(2,1)} %w_in.1, bf16[1536,384]{1,0:T(8,128)(2,1)} %w_out.1, bf16[16,384]{1,0:T(8,128)(2,1)} %cotangent.1), custom_call_target="tpu_custom_call" | custom-call | tf_op jit(solution)/shard_map/feed_forward/pallas_call | solution.py:302
  59.0 1.5 %place.1 = (bf16[16,384]{1,0:T(8,128)(2,1)}, bf16[16,384]{1,0:T(8,128)(2,1)}, bf16[384,1536]{1,0:T(8,128)(2,1)}, bf16[1536,384]{1,0:T(8,128)(2,1)}) custom-call(bf16[16,384]{1,0:T(8,128)(2,1)S(1)} %get-tuple-element.8.refs_0_, bf16[16,384]{1,0:T(8,128)(2,1)S(1)} %get-tuple-element.9.refs_1_, bf16[384,1536]{1,0:T(8,128)(2,1)S(1)} %get-tuple-element.10.refs_2_, ...), custom_call_target="tpu_custom_call" | custom-call | tf_op jit(solution)/shard_map/place/pallas_call | solution.py:338

commit v8 on v7

--- a/solution.py
+++ b/solution.py
@@ -117,14 +117,13 @@
         pltpu.make_async_copy(w_in.at[:, pl.ds(h * HALF, HALF)], w_in_v.at[h], load_sem.at[h])
         for h in range(2)
     ] + [pltpu.make_async_copy(w_out.at[pl.ds(h * HALF, HALF)], w_out_v.at[h], load_sem.at[2 + h]) for h in range(2)]
-    for copy in own + loads:
-        copy.start()
-
     barrier = pltpu.get_barrier_semaphore()
     peers = [across(step) for step in FAR_FIRST[:5]] + [along(offset) for offset in OFFSETS]
     peers += [across(step) for step in FAR_FIRST[5:]] + [twin]
     for peer in peers:
         pl.semaphore_signal(barrier, inc=1, device_id=peer, device_id_type=MESH)
+    for copy in own + loads:
+        copy.start()
     pl.semaphore_wait(barrier, len(peers))
 
     for k in range(2):
@@ -195,8 +194,11 @@
             for role in roles:
                 wait(units.at[k, c, rows(role), columns(q)], unit_recv.at[k, q, place_of(role)])
                 hand_out(k, q, role)
+                if role not in CHILDREN[q]:
+                    hand_over(k, q, role)
             for role in roles:
-                hand_over(k, q, role)
+                if role in CHILDREN[q]:
+                    hand_over(k, q, role)
 
     def unit_terms(k, group):
         blocks = (NEAR, FAR)[group]

time: 60.9 us -> 60.7 us (level)
  no operation moved by 1% of the time
where the time goes in v8:
time: 60.7 us; the launch traced here: 60.5 us
  Pallas kernels  59.8 us (99%)
  between operations  0.64 us (1%)
    pallas_call x1, Pallas kernels, exchange(): pl.pallas_call(kernel, out_shape=(pltpu.VMEM((BLOCK, DEPTH), bf16), pltpu...  58.3 us
    pallas_call x1, Pallas kernels, local(): pl.pallas_call(place, out_shape=tuple((pltpu.HBM(result.shape, result.dty...  1.49 us

profile of v8, /device:TPU:2, one launch (start us, length us, event | category | flops | bytes accessed | tf_op | source)
XLA Modules:
  0.0 60.5 jit_solution(7743064642648149055)
XLA Ops:
  0.6 58.3 %feed_forward.1 = (bf16[16,384]{1,0:T(8,128)(2,1)S(1)}, bf16[16,384]{1,0:T(8,128)(2,1)S(1)}, bf16[384,1536]{1,0:T(8,128)(2,1)S(1)}, bf16[1536,384]{1,0:T(8,128)(2,1)S(1)}) custom-call(bf16[16,384]{1,0:T(8,128)(2,1)} %inputs.1, bf16[384,1536]{1,0:T(8,128)(2,1)} %w_in.1, bf16[1536,384]{1,0:T(8,128)(2,1)} %w_out.1, bf16[16,384]{1,0:T(8,128)(2,1)} %cotangent.1), custom_call_target="tpu_custom_call" | custom-call | tf_op jit(solution)/shard_map/feed_forward/pallas_call | solution.py:304
  59.0 1.5 %place.1 = (bf16[16,384]{1,0:T(8,128)(2,1)}, bf16[16,384]{1,0:T(8,128)(2,1)}, bf16[384,1536]{1,0:T(8,128)(2,1)}, bf16[1536,384]{1,0:T(8,128)(2,1)}) custom-call(bf16[16,384]{1,0:T(8,128)(2,1)S(1)} %get-tuple-element.8.refs_0_, bf16[16,384]{1,0:T(8,128)(2,1)S(1)} %get-tuple-element.9.refs_1_, bf16[384,1536]{1,0:T(8,128)(2,1)S(1)} %get-tuple-element.10.refs_2_, ...), custom_call_target="tpu_custom_call" | custom-call | tf_op jit(solution)/shard_map/place/pallas_call | solution.py:340
